TPU v7x, 32 devices: a whole 2x2x4 slice. The times are simulated.
32 devices in a mesh: dp: 16 (over z, y, x), rep: 2 (over core).
Axes of the slice: x: 2, y: 2, z: 4, core: 2. Of those that a mesh axis runs over, the one named last changes fastest.
Arguments:
- media: bfloat16 [32, 5, 256, 1024], P(('dp', 'rep')), may hold values from -6 to 6
- latents: bfloat16 [32, 5, 64, 1024], P(('dp', 'rep')), may hold values from -6 to 6
- image_counts: int32 [32], P(('dp', 'rep')), may hold values from 1 to 5, as said below
- grad_out: bfloat16 [32, 5, 64, 1024], P(('dp', 'rep')), may hold values from -6 to 6
- media_gain: bfloat16 [1024], P('dp'), may hold values from 0.25 to 1.75
- media_bias: bfloat16 [1024], P('dp'), may hold values from -3 to 3
- latent_gain: bfloat16 [1024], P('dp'), may hold values from 0.25 to 1.75
- latent_bias: bfloat16 [1024], P('dp'), may hold values from -3 to 3
- feed_gain: bfloat16 [1024], P('dp'), may hold values from 0.25 to 1.75
- feed_bias: bfloat16 [1024], P('dp'), may hold values from -3 to 3
- query_weight: bfloat16 [1024, 512], P('dp'), may hold values from -0.1875 to 0.1875
- context_weight: bfloat16 [1024, 1024], P('dp'), may hold values from -0.1875 to 0.1875
- output_weight: bfloat16 [512, 1024], P('dp'), may hold values from -1.5 to 1.5
- up_weight: bfloat16 [1024, 4096], P('dp'), may hold values from -0.1875 to 0.1875
- down_weight: bfloat16 [4096, 1024], P('dp'), may hold values from -0.09375 to 0.09375
Outputs:
- latents_out: bfloat16 [32, 5, 64, 1024], P(('dp', 'rep'))
- grad_media: bfloat16 [32, 5, 256, 1024], P(('dp', 'rep'))
- grad_latents: bfloat16 [32, 5, 64, 1024], P(('dp', 'rep'))
- grad_media_gain: float32 [1024], P('dp')
- grad_media_bias: float32 [1024], P('dp')
- grad_latent_gain: float32 [1024], P('dp')
- grad_latent_bias: float32 [1024], P('dp')
- grad_feed_gain: float32 [1024], P('dp')
- grad_feed_bias: float32 [1024], P('dp')
- grad_query: float32 [1024, 512], P('dp')
- grad_context: float32 [1024, 1024], P('dp')
- grad_output: float32 [512, 1024], P('dp')
- grad_up: float32 [1024, 4096], P('dp')
- grad_down: float32 [4096, 1024], P('dp')
Inputs may be any that keep to these rules, and one draw needn't show every extreme that they name: Slot j of sample s holds an image where j < image_counts[s]; the other slots are empty. Some sample holds 5 images and some holds one.
All inputs are finite; a program needn't handle non-finite values.
Results may differ from a plain program's by a relative error of at most 0.014.
Values may be sent and summed in bfloat16 or wider, within the bound.
A program may use at most 192 MiB of HBM per device.

v0:
```python
import jax
import jax.numpy as jnp
from jax import lax
from jax.sharding import PartitionSpec as P

HEAD_DIM = 64


epsilon = 1e-05


def layer_norm(values, gain, offset):
    centre = jnp.mean(values, axis=-1, keepdims=True)
    shifted = values - centre
    spread = jnp.mean(shifted * shifted, axis=-1, keepdims=True)
    return shifted * lax.rsqrt(spread + epsilon) * gain + offset


def gelu_exact(values):
    return 0.5 * values * (1.0 + jax.scipy.special.erf(values * 0.7071067811865476))


def matmul(left, right):
    return jnp.dot(left, right, preferred_element_type=jnp.float32)


def matmul_left(left, right):
    return lax.dot_general(
        left, right, (((0,), (0,)), ((), ())), preferred_element_type=jnp.float32
    )


def matmul_right(left, right):
    return lax.dot_general(
        left, right, (((1,), (1,)), ((), ())), preferred_element_type=jnp.float32
    )


def head_scores(first_heads, second_heads):
    return jnp.einsum(
        "bqhd,bkhd->bhqk", first_heads, second_heads, preferred_element_type=jnp.float32
    )


def body(
    media,
    latents,
    image_counts,
    grad_out,
    media_gain,
    media_bias,
    latent_gain,
    latent_bias,
    feed_gain,
    feed_bias,
    query_weight,
    context_weight,
    output_weight,
    up_weight,
    down_weight,
):
    samples, slots, patches, model_width = media.shape
    latent_count = latents.shape[2]
    inner_width = query_weight.shape[1]
    head_count = inner_width // HEAD_DIM
    blocks = samples * slots
    key_count = patches + latent_count
    latent_total = blocks * latent_count
    scaling = HEAD_DIM ** (-0.5)
    gathered = (
        lax.all_gather(media_gain, "dp", axis=0, tiled=True),
        lax.all_gather(media_bias, "dp", axis=0, tiled=True),
        lax.all_gather(latent_gain, "dp", axis=0, tiled=True),
        lax.all_gather(latent_bias, "dp", axis=0, tiled=True),
        lax.all_gather(feed_gain, "dp", axis=0, tiled=True),
        lax.all_gather(feed_bias, "dp", axis=0, tiled=True),
        lax.all_gather(query_weight, "dp", axis=0, tiled=True),
        lax.all_gather(context_weight, "dp", axis=0, tiled=True),
        lax.all_gather(output_weight, "dp", axis=0, tiled=True),
        lax.all_gather(up_weight, "dp", axis=0, tiled=True),
        lax.all_gather(down_weight, "dp", axis=0, tiled=True),
    )
    vectors = [element.astype(jnp.float32) for element in gathered[:6]]
    media_rows = media.reshape(blocks * patches, model_width).astype(jnp.float32)
    latent_rows = latents.reshape(latent_total, model_width).astype(jnp.float32)
    media_normed = layer_norm(media_rows, vectors[0], vectors[1]).astype(jnp.bfloat16)
    latent_normed = layer_norm(latent_rows, vectors[2], vectors[3]).astype(jnp.bfloat16)
    queries = (matmul(latent_normed, gathered[6]) * scaling).astype(jnp.bfloat16)
    context = jnp.concatenate(
        [
            media_normed.reshape(blocks, patches, model_width),
            latent_normed.reshape(blocks, latent_count, model_width),
        ],
        axis=1,
    ).reshape(blocks * key_count, model_width)
    key_value = (
        matmul(context, gathered[7])
        .astype(jnp.bfloat16)
        .reshape(blocks, key_count, 2 * inner_width)
    )
    query_heads = queries.reshape(blocks, latent_count, head_count, HEAD_DIM)
    key_heads = key_value[:, :, :inner_width].reshape(blocks, key_count, head_count, HEAD_DIM)
    value_heads = key_value[:, :, inner_width:].reshape(blocks, key_count, head_count, HEAD_DIM)
    scores = head_scores(query_heads, key_heads)
    row_max = jnp.max(scores, axis=-1, keepdims=True)
    exponent = jnp.exp(scores - row_max)
    row_total = jnp.sum(exponent, axis=-1, keepdims=True)
    log_total = row_max + jnp.log(row_total)
    attention_weights = (exponent / row_total).astype(jnp.bfloat16)
    attended = (
        jnp.einsum(
            "bhqk,bkhd->bqhd", attention_weights, value_heads, preferred_element_type=jnp.float32
        )
        .astype(jnp.bfloat16)
        .reshape(latent_total, inner_width)
    )
    after_attention = latent_rows + matmul(attended, gathered[8])
    feed_input = layer_norm(after_attention, vectors[4], vectors[5]).astype(jnp.bfloat16)
    hidden = matmul(feed_input, gathered[9])
    activated = gelu_exact(hidden).astype(jnp.bfloat16)
    after_feed = after_attention + matmul(activated, gathered[10])
    slot_mask = (
        lax.broadcasted_iota(jnp.int32, (samples, slots), 1) < image_counts[:, None]
    ).astype(jnp.float32)
    row_mask = jnp.broadcast_to(slot_mask[:, :, None], (samples, slots, latent_count)).reshape(
        latent_total, 1
    )
    latents_out = (after_feed * row_mask).astype(jnp.bfloat16).reshape(latents.shape)
    backward_set = (
        lax.all_gather(media_gain, "dp", axis=0, tiled=True),
        lax.all_gather(media_bias, "dp", axis=0, tiled=True),
        lax.all_gather(latent_gain, "dp", axis=0, tiled=True),
        lax.all_gather(latent_bias, "dp", axis=0, tiled=True),
        lax.all_gather(feed_gain, "dp", axis=0, tiled=True),
        lax.all_gather(feed_bias, "dp", axis=0, tiled=True),
        lax.all_gather(query_weight, "dp", axis=0, tiled=True),
        lax.all_gather(context_weight, "dp", axis=0, tiled=True),
        lax.all_gather(output_weight, "dp", axis=0, tiled=True),
        lax.all_gather(up_weight, "dp", axis=0, tiled=True),
        lax.all_gather(down_weight, "dp", axis=0, tiled=True),
    )
    back_vectors = [element.astype(jnp.float32) for element in backward_set[:6]]
    d_after = grad_out.reshape(latent_total, model_width).astype(jnp.float32) * row_mask
    d_branch = d_after.astype(jnp.bfloat16)
    grad_down = matmul_left(activated, d_branch)
    d_activated = matmul_right(d_branch, backward_set[10])
    d_hidden = jax.vjp(gelu_exact, hidden)[1](d_activated)[0].astype(jnp.bfloat16)
    grad_up = matmul_left(feed_input, d_hidden)
    d_feed = matmul_right(d_hidden, backward_set[9])
    d_feed_norm, grad_feed_gain, grad_feed_bias = jax.vjp(
        layer_norm, after_attention, back_vectors[4], back_vectors[5]
    )[1](d_feed)
    d_middle = d_after + d_feed_norm
    d_out_branch = d_middle.astype(jnp.bfloat16)
    grad_output = matmul_left(attended, d_out_branch)
    d_attended = (
        matmul_right(d_out_branch, backward_set[8])
        .astype(jnp.bfloat16)
        .reshape(blocks, latent_count, head_count, HEAD_DIM)
    )
    recomputed = jnp.exp(head_scores(query_heads, key_heads) - log_total)
    d_weights = head_scores(d_attended, value_heads)
    d_scores = (
        recomputed * (d_weights - jnp.sum(recomputed * d_weights, axis=-1, keepdims=True))
    ).astype(jnp.bfloat16)
    d_queries = (
        jnp.einsum(
            "bhqk,bkhd->bqhd", d_scores, key_heads, preferred_element_type=jnp.float32
        ).astype(jnp.bfloat16)
        * scaling
    ).reshape(latent_total, inner_width)
    d_keys = jnp.einsum(
        "bhqk,bqhd->bkhd", d_scores, query_heads, preferred_element_type=jnp.float32
    ).astype(jnp.bfloat16)
    d_values = jnp.einsum(
        "bhqk,bqhd->bkhd",
        recomputed.astype(jnp.bfloat16),
        d_attended,
        preferred_element_type=jnp.float32,
    ).astype(jnp.bfloat16)
    d_key_value = jnp.concatenate(
        [
            d_keys.reshape(blocks, key_count, inner_width),
            d_values.reshape(blocks, key_count, inner_width),
        ],
        axis=-1,
    ).reshape(blocks * key_count, 2 * inner_width)
    grad_query = matmul_left(latent_normed, d_queries)
    grad_context = matmul_left(context, d_key_value)
    d_context = matmul_right(d_key_value, backward_set[7]).reshape(blocks, key_count, model_width)
    d_latent_normed = matmul_right(d_queries, backward_set[6]) + d_context[:, patches:, :].reshape(
        latent_total, model_width
    )
    d_media_normed = d_context[:, :patches, :].reshape(blocks * patches, model_width)
    d_latent_norm, grad_latent_gain, grad_latent_bias = jax.vjp(
        layer_norm, latent_rows, back_vectors[2], back_vectors[3]
    )[1](d_latent_normed)
    grad_latents = (d_middle + d_latent_norm).astype(jnp.bfloat16).reshape(latents.shape)
    d_media, grad_media_gain, grad_media_bias = jax.vjp(
        layer_norm, media_rows, back_vectors[0], back_vectors[1]
    )[1](d_media_normed)
    grad_media = d_media.astype(jnp.bfloat16).reshape(media.shape)
    partial_sums = (
        lax.psum_scatter(grad_media_gain, "dp", scatter_dimension=0, tiled=True),
        lax.psum_scatter(grad_media_bias, "dp", scatter_dimension=0, tiled=True),
        lax.psum_scatter(grad_latent_gain, "dp", scatter_dimension=0, tiled=True),
        lax.psum_scatter(grad_latent_bias, "dp", scatter_dimension=0, tiled=True),
        lax.psum_scatter(grad_feed_gain, "dp", scatter_dimension=0, tiled=True),
        lax.psum_scatter(grad_feed_bias, "dp", scatter_dimension=0, tiled=True),
        lax.psum_scatter(grad_query, "dp", scatter_dimension=0, tiled=True),
        lax.psum_scatter(grad_context, "dp", scatter_dimension=0, tiled=True),
        lax.psum_scatter(grad_output, "dp", scatter_dimension=0, tiled=True),
        lax.psum_scatter(grad_up, "dp", scatter_dimension=0, tiled=True),
        lax.psum_scatter(grad_down, "dp", scatter_dimension=0, tiled=True),
    )
    owned = (
        lax.psum(partial_sums[0].astype(jnp.bfloat16), "rep").astype(jnp.float32),
        lax.psum(partial_sums[1].astype(jnp.bfloat16), "rep").astype(jnp.float32),
        lax.psum(partial_sums[2].astype(jnp.bfloat16), "rep").astype(jnp.float32),
        lax.psum(partial_sums[3].astype(jnp.bfloat16), "rep").astype(jnp.float32),
        lax.psum(partial_sums[4].astype(jnp.bfloat16), "rep").astype(jnp.float32),
        lax.psum(partial_sums[5].astype(jnp.bfloat16), "rep").astype(jnp.float32),
        lax.psum(partial_sums[6].astype(jnp.bfloat16), "rep").astype(jnp.float32),
        lax.psum(partial_sums[7].astype(jnp.bfloat16), "rep").astype(jnp.float32),
        lax.psum(partial_sums[8].astype(jnp.bfloat16), "rep").astype(jnp.float32),
        lax.psum(partial_sums[9].astype(jnp.bfloat16), "rep").astype(jnp.float32),
        lax.psum(partial_sums[10].astype(jnp.bfloat16), "rep").astype(jnp.float32),
    )
    return (
        latents_out,
        grad_media,
        grad_latents,
        owned[0],
        owned[1],
        owned[2],
        owned[3],
        owned[4],
        owned[5],
        owned[6],
        owned[7],
        owned[8],
        owned[9],
        owned[10],
    )


def solution(mesh):
    return jax.shard_map(
        body,
        mesh=mesh,
        in_specs=(
            P(("dp", "rep"), None, None, None),
            P(("dp", "rep"), None, None, None),
            P(("dp", "rep")),
            P(("dp", "rep"), None, None, None),
            P("dp"),
            P("dp"),
            P("dp"),
            P("dp"),
            P("dp"),
            P("dp"),
            P("dp", None),
            P("dp", None),
            P("dp", None),
            P("dp", None),
            P("dp", None),
        ),
        out_specs=(
            P(("dp", "rep"), None, None, None),
            P(("dp", "rep"), None, None, None),
            P(("dp", "rep"), None, None, None),
            P("dp"),
            P("dp"),
            P("dp"),
            P("dp"),
            P("dp"),
            P("dp"),
            P("dp", None),
            P("dp", None),
            P("dp", None),
            P("dp", None),
            P("dp", None),
        ),
        check_vma=False,
    )
```

profile of v0, /device:TPU:0, one launch (start us, length us, event | category | flops | bytes accessed | tf_op | source)
XLA Modules:
  0.0 1523.6 jit_solution(11698806229793453673)
XLA Ops:
  17.6 78.7 %all-reduce.13 = (bf16[1024]{0:T(1024)(128)(2,1)S(1)}, bf16[1024]{0:T(1024)(128)(2,1)S(1)}, bf16[1024]{0:T(1024)(128)(2,1)S(1)}, bf16[1024]{0:T(1024)(128)(2,1)S...) all-reduce(bf16[1024]{0:T(1024)(128)(2,1)S(1)} %dynamic-update-slic, ...), channel_id=1, replica_groups=mesh['dp'=16,'rep'=2] {'dp'}, use_global_device_ids=true, to_apply=%add.3 | all-reduce | flops 6144 | bytes 24576
  102.8 2.1 pad_maximum_fusion
  107.6 2.5 fusion.39
  110.1 2.2 reshape.392
  112.3 2.3 copy.52
  114.5 17.0 %all-gather.6.cloned.1.call-done = bf16[1024,1024]{1,0:T(8,128)(2,1)} async-done(((bf16[64,1024]{1,0:T(8,128)(2,1)}), bf16[1024,1024]{1,0:T(8,128)(2,1)}) %all-gather.6.cloned.1.call-update) | async-done | bytes 2097168 | tf_op jit(solution)/shard_map/all_gather | solution.py:78
  131.5 6.2 convolution_convert_fusion
  137.7 2.1 fusion.53
  139.8 3.7 copy.47
  143.5 3.7 copy.48
  147.1 2.6 fusion.55
  152.7 2.3 fusion.36
  155.0 2.2 copy.50
  157.2 2.2 reshape.394
  159.5 28.8 %all-gather.10.cloned.1.call-done = bf16[512,1024]{1,0:T(8,128)(2,1)} async-done(((bf16[32,1024]{1,0:T(8,128)(2,1)}), bf16[512,1024]{1,0:T(8,128)(2,1)}) %all-gather.10.cloned.1.call-update) | async-done | bytes 1048592 | tf_op jit(solution)/shard_map/all_gather | solution.py:79
  191.5 111.0 %all-gather.12.cloned.1.call-done = bf16[1024,4096]{1,0:T(8,128)(2,1)} async-done(((bf16[64,4096]{1,0:T(8,128)(2,1)}), bf16[1024,4096]{1,0:T(8,128)(2,1)}) %all-gather.12.cloned.1.call-update) | async-done | bytes 8388624 | tf_op jit(solution)/shard_map/all_gather | solution.py:80
  302.5 9.1 fusion.51
  311.7 104.5 %all-gather.14.cloned.1.call-done = bf16[4096,1024]{1,0:T(8,128)(2,1)} async-done(((bf16[256,1024]{1,0:T(8,128)(2,1)}), bf16[4096,1024]{1,0:T(8,128)(2,1)}) %all-gather.14.cloned.1.call-update) | async-done | bytes 8388624 | tf_op jit(solution)/shard_map/all_gather | solution.py:81
  416.2 9.7 add_convert_fusion
  427.4 3.2 multiply_reduce_fusion.1
  434.6 2.2 reshape.396
  436.8 2.3 copy.53
  439.1 4.6 multiply_reduce_fusion
  447.6 2.3 copy.56
  449.9 2.2 reshape.397
  452.1 3.2 fusion.58
  455.5 3.3 fusion.59
  458.8 4.5 fusion.24
  463.3 4.0 copy.55
  467.3 3.7 convolution_convert_fusion.1
  471.0 3.9 copy.54
  474.9 8.9 convolution_bitcast_fusion
  483.9 12.6 fusion.50
  496.7 12.2 fusion.60
  509.6 5.9 fusion.18
  521.8 3.7 fusion.4
  526.3 2.8 fusion.15
  529.1 2.9 fusion.6
  532.0 2.2 reduce-scatter.6.cloned.1.call-done
  535.7 79.0 %reduce-scatter.10.cloned.1.call-done = f32[32,1024]{1,0:T(8,128)} async-done(((f32[512,1024]{1,0:T(8,128)}), f32[32,1024]{1,0:T(8,128)}) %reduce-scatter.10.cloned.1.call-update) | async-done | bytes 131088 | tf_op jit(solution)/shard_map/reduce_scatter | solution.py:212
  616.2 92.7 %reduce-scatter.8.cloned.1.call-done = f32[64,1024]{1,0:T(8,128)} async-done(((f32[1024,1024]{1,0:T(8,128)}), f32[64,1024]{1,0:T(8,128)}) %reduce-scatter.8.cloned.1.call-update) | async-done | bytes 262160 | tf_op jit(solution)/shard_map/reduce_scatter | solution.py:211
  710.5 346.7 %reduce-scatter.12.cloned.1.call-done = f32[64,4096]{1,0:T(8,128)} async-done(((f32[1024,4096]{1,0:T(8,128)}), f32[64,4096]{1,0:T(8,128)}) %reduce-scatter.12.cloned.1.call-update) | async-done | bytes 1048592 | tf_op jit(solution)/shard_map/reduce_scatter | solution.py:213
  1059.3 352.1 %reduce-scatter.14.cloned.1.call-done = f32[256,1024]{1,0:T(8,128)} async-done(((f32[4096,1024]{1,0:T(8,128)}), f32[256,1024]{1,0:T(8,128)}) %reduce-scatter.14.cloned.1.call-update) | async-done | bytes 1048592 | tf_op jit(solution)/shard_map/reduce_scatter | solution.py:214
  1411.4 2.1 convert_element_type.277
  1413.6 79.4 %all-reduce.12 = (bf16[1024]{0:T(1024)(128)(2,1)S(1)}, bf16[1024]{0:T(1024)(128)(2,1)S(1)}, bf16[1024]{0:T(1024)(128)(2,1)S(1)}, bf16[1024]{0:T(1024)(128)(2,1)S...) all-reduce(f32[1024]{0:T(1024)S(1)} %get-tuple-element.14, ...), channel_id=2, replica_groups=mesh['dp'=16,'rep'=2] {'dp'}, use_global_device_ids=true, to_apply=%region_16.0.clone | all-reduce | flops 6144 | bytes 36864
  1493.4 2.7 all-reduce.14
  1499.2 2.5 add_convert_fusion.2
  1501.7 7.1 fusion.28
  (157 shorter events, 59.3 us)
Async XLA Ops:
  7.2 92.9 %copy-start.2 = (bf16[1,5,256,1024]{3,2,1,0:T(8,128)(2,1)S(1)}, bf16[1,5,256,1024]{3,2,1,0:T(8,128)(2,1)}, u32[]{:S(2)}) copy-start(bf16[1,5,256,1024]{3,2,1,0:T(8,128)(2,1)} %param.15) | copy-start | bytes 7864324
  7.2 100.4 %all-gather.8.cloned.1.call-start = ((), (), s32[]{:S(2)}) async-start(), calls=%async_computation.6 | async-start | bytes 1114112 | tf_op jit(solution)/shard_map/all_gather | solution.py:77
  7.9 123.6 %all-gather.6.cloned.1.call-start = ((), (), s32[]{:S(2)}) async-start(), calls=%async_computation.5 | async-start | bytes 2228224 | tf_op jit(solution)/shard_map/all_gather | solution.py:78
  8.7 179.6 %all-gather.10.cloned.1.call-start = ((), (), s32[]{:S(2)}) async-start(), calls=%async_computation.7 | async-start | bytes 1114112 | tf_op jit(solution)/shard_map/all_gather | solution.py:79
  9.4 293.1 %all-gather.12.cloned.1.call-start = ((), (), s32[]{:S(2)}) async-start(), calls=%async_computation.8 | async-start | bytes 8912896 | tf_op jit(solution)/shard_map/all_gather | solution.py:80
  10.0 406.2 %all-gather.14.cloned.1.call-start = ((), (), s32[]{:S(2)}) async-start(), calls=%async_computation.9 | async-start | bytes 8912896 | tf_op jit(solution)/shard_map/all_gather | solution.py:81
  10.6 523.6 %reduce-scatter.6.cloned.1.call-start = ((), (), s32[]{:S(2)}) async-start(), calls=%async_computation.10 | async-start | bytes 2228224 | tf_op jit(solution)/shard_map/reduce_scatter | solution.py:210
  100.0 1.3 copy-start.5
  101.6 1.1 copy-start.20
  102.8 2.6 copy-start.13
  102.8 2.6 copy-start.15
  149.7 2.0 copy-start
  149.7 3.0 copy-start.14
  190.2 1.0 copy-start.6
  416.2 11.2 copy-start.7
  416.2 11.2 copy-start.25
  425.9 1.5 copy-start.19
  430.6 1.6 copy-start.16
  430.7 2.7 copy-start.23
  431.1 1.1 copy-start.11
  432.5 0.9 copy-start.21
  439.1 4.6 copy-start.1
  443.7 2.3 copy-start.9
  444.7 1.3 copy-start.10
  455.4 159.2 %reduce-scatter.10.cloned.1.call-start = ((), (), s32[]{:S(2)}) async-start(), calls=%async_computation.12 | async-start | bytes 2228224 | tf_op jit(solution)/shard_map/reduce_scatter | solution.py:212
  458.8 250.1 %reduce-scatter.8.cloned.1.call-start = ((), (), s32[]{:S(2)}) async-start(), calls=%async_computation.11 | async-start | bytes 4456448 | tf_op jit(solution)/shard_map/reduce_scatter | solution.py:211
  483.8 573.4 %reduce-scatter.12.cloned.1.call-start = ((), (), s32[]{:S(2)}) async-start(), calls=%async_computation.13 | async-start | bytes 17825792 | tf_op jit(solution)/shard_map/reduce_scatter | solution.py:213
  496.4 915.0 %reduce-scatter.14.cloned.1.call-start = ((), (), s32[]{:S(2)}) async-start(), calls=%async_computation.14 | async-start | bytes 17825792 | tf_op jit(solution)/shard_map/reduce_scatter | solution.py:214
  508.9 999.9 %all-reduce.18.cloned.1.call-start = ((), (), s32[]{:S(2)}) async-start(), calls=%async_computation.15 | async-start | bytes 2621440 | tf_op jit(solution)/shard_map/psum | solution.py:223
  515.5 3.3 copy-start.3
  515.6 1.2 copy-start.22
  515.6 2.3 copy-start.26
  521.8 4.5 copy-start.4
  535.7 963.5 %copy-start.12 = (f32[320,1024]{1,0:T(8,128)S(1)}, f32[320,1024]{1,0:T(8,128)}, u32[]{:S(2)}) copy-start(f32[320,1024]{1,0:T(8,128)} %copy-done.11) | copy-start | bytes 3932164
  535.7 963.5 %copy-start.17 = (bf16[1,5,64,1024]{3,2,1,0:T(8,128)(2,1)S(1)}, bf16[1,5,64,1024]{3,2,1,0:T(8,128)(2,1)}, u32[]{:S(2)}) copy-start(bf16[1,5,64,1024]{3,2,1,0:T(8,128)(2,1)} %param.18) | copy-start | bytes 1966084
  1413.5 88.2 %copy-start.8 = (f32[320,1024]{1,0:T(8,128)S(1)}, f32[320,1024]{1,0:T(8,128)}, u32[]{:S(2)}) copy-start(f32[320,1024]{1,0:T(8,128)} %copy-done.6) | copy-start | bytes 3932164
  1496.1 5.6 copy-start.18
  1508.8 6.8 copy-start.24
Sparse Core Ops, SparseCore 0:
  10.8 58.1 all-gather.7
  71.7 59.7 all-gather.5
  134.3 53.9 all-gather.9
  190.9 111.6 all-gather.11
  305.2 111.0 all-gather.13
  455.5 78.5 reduce-scatter.5
  536.4 78.1 reduce-scatter.9
  616.9 91.9 reduce-scatter.7
  711.2 345.9 reduce-scatter.11
  1059.4 352.0 reduce-scatter.13
  1414.7 25.8 all-reduce.17
where the time goes:
time: 1530 us; the launch traced here: 1520 us
  waiting for transfers between devices  1140 us (75%)
  blocking collectives  161 us (11%)
  matrix products  107 us (7%)
  local copies, waits for them, and re-layouts  53.4 us (3%)
  other arithmetic  47.5 us (3%)
  between operations  16.7 us (1%)
    reduce_scatter x1, waiting for transfers between devices, body(): lax.psum_scatter(grad_down, 'dp', scatter_dimension=0, tiled=True)  352 us
    reduce_scatter x1, waiting for transfers between devices, body(): lax.psum_scatter(grad_up, 'dp', scatter_dimension=0, tiled=True)  347 us
    unnamed x2, blocking collectives  158 us
    all_gather x1, waiting for transfers between devices, body(): lax.all_gather(up_weight, 'dp', axis=0, tiled=True)  111 us
    all_gather x1, waiting for transfers between devices, body(): lax.all_gather(down_weight, 'dp', axis=0, tiled=True)  105 us
    reduce_scatter x1, waiting for transfers between devices, body(): lax.psum_scatter(grad_context, 'dp', scatter_dimension=0, tiled=True)  92.7 us
    reduce_scatter x1, waiting for transfers between devices, body(): lax.psum_scatter(grad_output, 'dp', scatter_dimension=0, tiled=True)  79 us
    dot_general x5, matrix products, matmul_left(): lax.dot_general(left, right, (((0,), (0,)), ((), ())), preferred_element_...  40.2 us
  transfers between devices with their start and end apart: 11, of which 9 were waited for; matrix products, arithmetic and copies ran while one was open for 10% of the time, Pallas kernels for 0%

commit v1 on v0

--- a/solution.py
+++ b/solution.py
@@ -1,6 +1,10 @@
+import functools
+
 import jax
 import jax.numpy as jnp
 from jax import lax
+from jax.experimental import pallas as pl
+from jax.experimental.pallas import tpu as pltpu
 from jax.sharding import PartitionSpec as P
 
 HEAD_DIM = 64
@@ -8,6 +12,429 @@
 
 epsilon = 1e-05
 
+MESH = pl.DeviceIdType.MESH
+ALL = slice(None)
+
+
+class Links:
+    def __init__(self, length):
+        self.length = length
+        self.dp = lax.axis_index("dp")
+        self.rep = lax.axis_index("rep")
+        self.z = lax.div(self.dp, 4)
+        self.y = lax.rem(lax.div(self.dp, 2), 2)
+        self.x = lax.rem(self.dp, 2)
+
+    def device(self, axis, way=0):
+        if axis == "core":
+            return (self.dp, 1 - self.rep)
+        if axis == "x":
+            return (self.dp + 1 - 2 * self.x, self.rep)
+        if axis == "y":
+            return (self.dp + 2 - 4 * self.y, self.rep)
+        return (self.dp + 4 * way, self.rep)
+
+    def greet(self):
+        barrier = pltpu.get_barrier_semaphore()
+        for axis in ("core", "x", "y"):
+            pl.semaphore_signal(barrier, inc=1, device_id=self.device(axis), device_id_type=MESH)
+
+        @pl.when(self.z > 0)
+        def _():
+            pl.semaphore_signal(barrier, inc=1, device_id=self.device("z", -1), device_id_type=MESH)
+
+        @pl.when(self.z < self.length - 1)
+        def _():
+            pl.semaphore_signal(barrier, inc=1, device_id=self.device("z", 1), device_id_type=MESH)
+
+        inside = jnp.where(self.z > 0, 1, 0) + jnp.where(self.z < self.length - 1, 1, 0)
+        pl.semaphore_wait(barrier, 3 + inside)
+
+
+class Move:
+    def __init__(self, send, recv, slot, device, source, target, landing, gives=None, takes=None):
+        self.out = pltpu.make_async_remote_copy(
+            src_ref=source, dst_ref=target, send_sem=send.at[slot], recv_sem=recv.at[slot],
+            device_id=device, device_id_type=MESH)
+        self.into = pltpu.make_async_remote_copy(
+            src_ref=landing, dst_ref=landing, send_sem=send.at[slot], recv_sem=recv.at[slot],
+            device_id=device, device_id_type=MESH)
+        self.gives, self.takes = gives, takes
+
+    def start(self):
+        guarded(self.gives, self.out.start)
+
+    def wait(self, then=None):
+        def both():
+            self.into.wait_recv()
+            if then is not None:
+                then()
+
+        guarded(self.takes, both)
+
+    def drain(self):
+        guarded(self.gives, self.out.wait_send)
+
+
+def guarded(condition, action):
+    if condition is None:
+        action()
+    else:
+        pl.when(condition)(action)
+
+
+class Slots:
+    def __init__(self, send, recv):
+        self.send, self.recv, self.used = send, recv, 0
+
+    def take(self):
+        self.used += 1
+        return self.used - 1
+
+    def move(self, *args, **kwargs):
+        return Move(self.send, self.recv, self.take(), *args, **kwargs)
+
+
+class Gather:
+    def __init__(self, links, slots, view, order, halved):
+        self.moves = []
+        z, y, x, length = links.z, links.y, links.x, links.length
+        here = {"z": z, "y": y, "x": x}
+        for hop in range(1, length):
+            up = view(z - hop + 1, y, x)
+            down = view(z + hop - 1, y, x)
+            self.moves.append([
+                slots.move(links.device("z", 1), up, up, view(z - hop, y, x),
+                           gives=(z < length - 1) & (z >= hop - 1), takes=z >= hop),
+                slots.move(links.device("z", -1), down, down, view(z + hop, y, x),
+                           gives=(z > 0) & (z + hop <= length), takes=z + hop < length),
+            ])
+        here["z"] = ALL
+        for axis in order:
+            mine = view(here["z"], here["y"], here["x"])
+            other = dict(here)
+            other[axis] = 1 - here[axis]
+            self.moves.append([
+                slots.move(links.device(axis), mine, mine, view(other["z"], other["y"], other["x"]))])
+            here[axis] = ALL
+        if halved:
+            mine = view(ALL, ALL, ALL)
+            self.moves.append([
+                slots.move(links.device("core"), mine, mine, view(ALL, ALL, ALL, 1 - links.rep))])
+
+    def step(self, number):
+        if 0 < number <= len(self.moves):
+            for move in self.moves[number - 1]:
+                move.wait()
+        if number < len(self.moves):
+            for move in self.moves[number]:
+                move.start()
+
+    def drain(self):
+        for group in self.moves:
+            for move in group:
+                move.drain()
+
+
+class Reduce:
+    def __init__(self, links, slots, own, order, lands_b, lands_a, lands_z, finish):
+        self.own, self.order, self.links, self.finish = own, order, links, finish
+        self.moves, self.adds = [], []
+        z, y, x, length = links.z, links.y, links.x, links.length
+        here = {"z": ALL, "y": ALL, "x": ALL}
+        for axis, lands in zip(order, (lands_b, lands_a)):
+            away, home = dict(here), dict(here)
+            place = {"y": y, "x": x}[axis]
+            away[axis], home[axis] = 1 - place, place
+            self.moves.append([slots.move(
+                links.device(axis), own(away["z"], away["y"], away["x"]), lands, lands)])
+            here = home
+            self.adds.append([functools.partial(add_into, own(home["z"], home["y"], home["x"]), lands)])
+        for hop in range(1, length):
+            above, below = z + length - hop, z - length + hop
+            from_below, from_above = lands_z.at[0, hop - 1], lands_z.at[1, hop - 1]
+            last = hop == length - 1
+            self.moves.append([
+                slots.move(links.device("z", 1), own(above, y, x), from_below, from_below,
+                           gives=(z < length - 1) & (z < hop), takes=(z > 0) & (z <= hop)),
+                slots.move(links.device("z", -1), own(below, y, x), from_above, from_above,
+                           gives=(z > 0) & (z >= length - hop),
+                           takes=(z < length - 1) & (z >= length - 1 - hop)),
+            ])
+            if last:
+                self.adds.append([None, None])
+            else:
+                self.adds.append([
+                    functools.partial(add_into, own(above - 1, y, x), from_below),
+                    functools.partial(add_into, own(below + 1, y, x), from_above)])
+        self.lands_z = lands_z
+
+    def step(self, number):
+        if 0 < number <= len(self.moves):
+            for move, add in zip(self.moves[number - 1], self.adds[number - 1]):
+                move.wait(add)
+            if number == len(self.moves):
+                self.end()
+        if number < len(self.moves):
+            for move in self.moves[number]:
+                move.start()
+
+    def end(self):
+        links, length = self.links, self.links.length
+        block = self.own(links.z, links.y, links.x)
+
+        def total(below, above):
+            value = block[...].astype(jnp.float32)
+            if below:
+                value = value + self.lands_z[0, length - 2].astype(jnp.float32)
+            if above:
+                value = value + self.lands_z[1, length - 2].astype(jnp.float32)
+            self.finish(value)
+
+        pl.when(links.z == 0)(lambda: total(False, True))
+        pl.when(links.z == length - 1)(lambda: total(True, False))
+        pl.when((links.z > 0) & (links.z < length - 1))(lambda: total(True, True))
+
+    def drain(self):
+        for group in self.moves:
+            for move in group:
+                move.drain()
+
+
+def add_into(target, arrived):
+    lead = target.shape[:-2]
+    if not lead:
+        target[...] = (target[...].astype(jnp.float32) + arrived[...].astype(jnp.float32)).astype(target.dtype)
+        return
+    count = 1
+    for size in lead:
+        count *= size
+
+    @pl.loop(0, count)
+    def _(flat):
+        index = []
+        for size in reversed(lead):
+            index.insert(0, lax.rem(flat, size))
+            flat = lax.div(flat, size)
+        index = tuple(index)
+        target[index] = (target[index].astype(jnp.float32) + arrived[index].astype(jnp.float32)).astype(target.dtype)
+
+
+def gather_kernel(length, *refs):
+    names = 5
+    shards, packed = refs[:names], refs[names]
+    outs, packed_out = refs[names + 1:2 * names + 1], refs[2 * names + 1]
+    send, recv, local = refs[2 * names + 2:]
+    links = Links(length)
+    z, y, x, rep = links.z, links.y, links.x, links.rep
+    staged = []
+    for number, (shard, out) in enumerate(zip(shards, outs)):
+        rows = out.shape[-2]
+        staged.append(pltpu.make_async_copy(
+            shard.at[pl.ds(pl.multiple_of(rep * rows, 16), rows)], out.at[z, y, x, rep], local.at[number]))
+    staged.append(pltpu.make_async_copy(packed, packed_out.at[z, y, x], local.at[names]))
+    for copy in staged:
+        copy.start()
+    links.greet()
+    slots = Slots(send, recv)
+    items = []
+
+    def window(out, begin, width):
+        def view(zi, yi, xi, half=rep):
+            return out.at[zi, yi, xi, half, :, pl.ds(begin, width)]
+
+        return view
+
+    def pair(out, begin, width):
+        return [Gather(links, slots, window(out, begin, width), ("x", "y"), True),
+                Gather(links, slots, window(out, begin + width, width), ("y", "x"), True)]
+
+    query, context, output, up, down = outs
+    items.append([Gather(links, slots, lambda zi, yi, xi: packed_out.at[zi, yi, xi], ("x", "y"), False)]
+                 + pair(context, 0, context.shape[-1] // 2))
+    items.append(pair(query, 0, query.shape[-1] // 2) + pair(output, 0, output.shape[-1] // 2))
+    quarter = up.shape[-1] // 4
+    items.append(pair(up, 0, quarter))
+    items.append(pair(up, 2 * quarter, quarter))
+    quarter = down.shape[-1] // 4
+    items.append(pair(down, 0, quarter))
+    items.append(pair(down, 2 * quarter, quarter))
+    for copy in staged:
+        copy.wait()
+    depth = length + 3
+    for tick in range(len(items) + depth - 1):
+        for number in range(len(items)):
+            step = tick - number
+            if 0 <= step < depth:
+                for gather in items[number]:
+                    gather.step(step)
+    for item in items:
+        for gather in item:
+            gather.drain()
+
+
+def reduce_kernel(length, grads, vectors, outs, vectors_out, own, lands_c, lands_b, lands_a, lands_z, result,
+                  vector_lands, send, recv, local):
+    links = Links(length)
+    z, y, x, rep = links.z, links.y, links.x, links.rep
+    loads = []
+    for number, (grad, mine) in enumerate(zip(grads, own)):
+        loads.append(pltpu.make_async_copy(grad.at[:, :, :, rep], mine, local.at[number]))
+        loads[-1].start()
+    links.greet()
+    slots = Slots(send, recv)
+    siblings = [slots.move(links.device("core"), grad.at[:, :, :, 1 - rep], land, land)
+                for grad, land in zip(grads, lands_c)]
+    steps = []
+
+    def pair(number, begin, width):
+        made = []
+        for order, first in ((("y", "x"), begin), (("x", "y"), begin + width)):
+            window = pl.ds(first, width)
+
+            def view(zi, yi, xi, window=window):
+                return own[number].at[zi, yi, xi, :, window]
+
+            def finish(value, window=window):
+                result[number][:, window] = value
+
+            made.append(Reduce(
+                links, slots, view, order, lands_b[number].at[:, :, :, window], lands_a[number].at[:, :, window],
+                lands_z[number].at[:, :, :, window], finish))
+        return made
+
+    order = (4, 3, 1, 0, 2)
+    for number in order:
+        siblings[number].start()
+    items = []
+    for number in order:
+        width = own[number].shape[-1]
+        parts = 2 if number >= 3 else 1
+        width //= 2 * parts
+        for part in range(parts):
+            items.append((number, part == 0, pair(number, 2 * part * width, width)))
+    vectors_out[...] = vectors[...]
+    for axis in ("core", "x", "y"):
+        number = ("core", "x", "y").index(axis)
+        mine, land = vector_lands.at[2 * number], vector_lands.at[2 * number + 1]
+        mine[...] = vectors_out[...]
+        move = slots.move(links.device(axis), mine, land, land)
+        move.start()
+        move.wait()
+        vectors_out[...] = mine[...] + land[...]
+        move.drain()
+    base = 6
+    running = vector_lands.at[base]
+    running[...] = vectors_out[...]
+    line = []
+    for hop in range(1, length):
+        mine_up, mine_down = vector_lands.at[base + 4 * hop - 3], vector_lands.at[base + 4 * hop - 2]
+        below, above = vector_lands.at[base + 4 * hop - 1], vector_lands.at[base + 4 * hop]
+        if hop == 1:
+            mine_up[...] = running[...]
+            mine_down[...] = running[...]
+        else:
+            mine_up[...] = vector_lands[base + 4 * hop - 5]
+            mine_down[...] = vector_lands[base + 4 * hop - 4]
+        moves = [
+            slots.move(links.device("z", 1), mine_up, below, below,
+                       gives=(z < length - 1) & (z >= hop - 1), takes=z >= hop),
+            slots.move(links.device("z", -1), mine_down, above, above,
+                       gives=(z > 0) & (z + hop <= length), takes=z + hop < length)]
+        for move in moves:
+            move.start()
+
+        def take(land):
+            vectors_out[...] = vectors_out[...] + land[...]
+
+        moves[0].wait(functools.partial(take, below))
+        moves[1].wait(functools.partial(take, above))
+        line += moves
+    depth = length + 2
+    for tick in range(len(items) + depth - 1):
+        for place, (number, first, halves) in enumerate(items):
+            step = tick - place
+            if step == 0 and first:
+                loads[number].wait()
+                siblings[number].wait()
+                add_into(own[number], lands_c[number])
+            if 0 <= step < depth:
+                for half in halves:
+                    half.step(step)
+    finals = []
+    for number, (total, out) in enumerate(zip(result, outs)):
+        keep = pltpu.make_async_copy(total, out.at[rep], local.at[number])
+        keep.start()
+        move = slots.move(links.device("core"), total, out.at[rep], out.at[1 - rep])
+        move.start()
+        finals.append((keep, move))
+    for keep, move in finals:
+        keep.wait()
+        move.wait()
+        move.drain()
+    for move in siblings + line:
+        move.drain()
+    for number, first, halves in items:
+        for half in halves:
+            half.drain()
+
+
+def gather_parameters(shards, packed, length):
+    blocks = (length, 2, 2)
+    anywhere = pl.BlockSpec(memory_space=pl.ANY)
+    out_shape = [jax.ShapeDtypeStruct(blocks + (2, s.shape[0] // 2, s.shape[1]), s.dtype) for s in shards]
+    out_shape.append(jax.ShapeDtypeStruct(blocks + packed.shape, packed.dtype))
+    made = pl.pallas_call(
+        functools.partial(gather_kernel, length),
+        out_shape=out_shape,
+        in_specs=[anywhere] * (len(shards) + 1),
+        out_specs=[anywhere] * (len(shards) + 1),
+        scratch_shapes=[
+            pltpu.SemaphoreType.DMA((160,)),
+            pltpu.SemaphoreType.DMA((160,)),
+            pltpu.SemaphoreType.DMA((8,)),
+        ],
+        compiler_params=pltpu.CompilerParams(collective_id=0, has_side_effects=True),
+        name="gather_parameters",
+    )(*shards, packed)
+    return [m.reshape(-1, m.shape[-1]) for m in made[:-1]], made[-1]
+
+
+def reduce_gradients(grads, vectors, length):
+    blocks = (length, 2, 2)
+    anywhere = pl.BlockSpec(memory_space=pl.ANY)
+    count = len(grads)
+    folded = []
+    for grad in grads:
+        rows = grad.shape[0] // (8 * length)
+        folded.append(grad.reshape(blocks + (2, rows, grad.shape[1])))
+    halves = [f.shape[4:] for f in folded]
+    bf16 = jnp.bfloat16
+    scratch = [
+        [pltpu.VMEM(blocks + h, bf16) for h in halves],
+        [pltpu.VMEM(blocks + h, bf16) for h in halves],
+        [pltpu.VMEM((length, 2) + h, bf16) for h in halves],
+        [pltpu.VMEM((length,) + h, bf16) for h in halves],
+        [pltpu.VMEM((2, length - 1) + h, bf16) for h in halves],
+        [pltpu.VMEM(h, jnp.float32) for h in halves],
+        pltpu.VMEM((6 + 4 * length,) + vectors.shape, jnp.float32),
+        pltpu.SemaphoreType.DMA((200,)),
+        pltpu.SemaphoreType.DMA((200,)),
+        pltpu.SemaphoreType.DMA((8,)),
+    ]
+    vmem = pl.BlockSpec(memory_space=pltpu.VMEM)
+    outs, vectors_out = pl.pallas_call(
+        functools.partial(reduce_kernel, length),
+        out_shape=([jax.ShapeDtypeStruct((2,) + h, jnp.float32) for h in halves],
+                   jax.ShapeDtypeStruct(vectors.shape, jnp.float32)),
+        in_specs=[[anywhere] * count, vmem],
+        out_specs=([anywhere] * count, vmem),
+        scratch_shapes=scratch,
+        compiler_params=pltpu.CompilerParams(
+            collective_id=1, has_side_effects=True, vmem_limit_bytes=56 * 2 ** 20),
+        name="reduce_gradients",
+    )(folded, vectors)
+    return [o.reshape(-1, o.shape[-1]) for o in outs], vectors_out
 
 def layer_norm(values, gain, offset):
     centre = jnp.mean(values, axis=-1, keepdims=True)
@@ -67,19 +494,18 @@
     key_count = patches + latent_count
     latent_total = blocks * latent_count
     scaling = HEAD_DIM ** (-0.5)
-    gathered = (
-        lax.all_gather(media_gain, "dp", axis=0, tiled=True),
-        lax.all_gather(media_bias, "dp", axis=0, tiled=True),
-        lax.all_gather(latent_gain, "dp", axis=0, tiled=True),
-        lax.all_gather(latent_bias, "dp", axis=0, tiled=True),
-        lax.all_gather(feed_gain, "dp", axis=0, tiled=True),
-        lax.all_gather(feed_bias, "dp", axis=0, tiled=True),
-        lax.all_gather(query_weight, "dp", axis=0, tiled=True),
-        lax.all_gather(context_weight, "dp", axis=0, tiled=True),
-        lax.all_gather(output_weight, "dp", axis=0, tiled=True),
-        lax.all_gather(up_weight, "dp", axis=0, tiled=True),
-        lax.all_gather(down_weight, "dp", axis=0, tiled=True),
-    )
+    vector_shards = (media_gain, media_bias, latent_gain, latent_bias, feed_gain, feed_bias)
+    weight_shards = (query_weight, context_weight, output_weight, up_weight, down_weight)
+    chips = lax.axis_size("dp")
+    tiled = chips % 4 == 0 and chips > 4 and all(s.shape[0] % 32 == 0 for s in weight_shards)
+    if tiled:
+        packed = jnp.pad(jnp.stack(vector_shards), ((0, 10), (0, 128 - media_gain.shape[0])))
+        matrices, packed = gather_parameters(weight_shards, packed, chips // 4)
+        packed = packed.reshape(chips, 16, 128)[:, :6, :media_gain.shape[0]]
+        gathered = tuple(packed.transpose(1, 0, 2).reshape(6, model_width)) + tuple(matrices)
+    else:
+        gathered = tuple(
+            lax.all_gather(s, "dp", axis=0, tiled=True) for s in vector_shards + weight_shards)
     vectors = [element.astype(jnp.float32) for element in gathered[:6]]
     media_rows = media.reshape(blocks * patches, model_width).astype(jnp.float32)
     latent_rows = latents.reshape(latent_total, model_width).astype(jnp.float32)
@@ -126,19 +552,7 @@
         latent_total, 1
     )
     latents_out = (after_feed * row_mask).astype(jnp.bfloat16).reshape(latents.shape)
-    backward_set = (
-        lax.all_gather(media_gain, "dp", axis=0, tiled=True),
-        lax.all_gather(media_bias, "dp", axis=0, tiled=True),
-        lax.all_gather(latent_gain, "dp", axis=0, tiled=True),
-        lax.all_gather(latent_bias, "dp", axis=0, tiled=True),
-        lax.all_gather(feed_gain, "dp", axis=0, tiled=True),
-        lax.all_gather(feed_bias, "dp", axis=0, tiled=True),
-        lax.all_gather(query_weight, "dp", axis=0, tiled=True),
-        lax.all_gather(context_weight, "dp", axis=0, tiled=True),
-        lax.all_gather(output_weight, "dp", axis=0, tiled=True),
-        lax.all_gather(up_weight, "dp", axis=0, tiled=True),
-        lax.all_gather(down_weight, "dp", axis=0, tiled=True),
-    )
+    backward_set = gathered
     back_vectors = [element.astype(jnp.float32) for element in backward_set[:6]]
     d_after = grad_out.reshape(latent_total, model_width).astype(jnp.float32) * row_mask
     d_branch = d_after.astype(jnp.bfloat16)
@@ -200,32 +614,20 @@
         layer_norm, media_rows, back_vectors[0], back_vectors[1]
     )[1](d_media_normed)
     grad_media = d_media.astype(jnp.bfloat16).reshape(media.shape)
-    partial_sums = (
-        lax.psum_scatter(grad_media_gain, "dp", scatter_dimension=0, tiled=True),
-        lax.psum_scatter(grad_media_bias, "dp", scatter_dimension=0, tiled=True),
-        lax.psum_scatter(grad_latent_gain, "dp", scatter_dimension=0, tiled=True),
-        lax.psum_scatter(grad_latent_bias, "dp", scatter_dimension=0, tiled=True),
-        lax.psum_scatter(grad_feed_gain, "dp", scatter_dimension=0, tiled=True),
-        lax.psum_scatter(grad_feed_bias, "dp", scatter_dimension=0, tiled=True),
-        lax.psum_scatter(grad_query, "dp", scatter_dimension=0, tiled=True),
-        lax.psum_scatter(grad_context, "dp", scatter_dimension=0, tiled=True),
-        lax.psum_scatter(grad_output, "dp", scatter_dimension=0, tiled=True),
-        lax.psum_scatter(grad_up, "dp", scatter_dimension=0, tiled=True),
-        lax.psum_scatter(grad_down, "dp", scatter_dimension=0, tiled=True),
-    )
-    owned = (
-        lax.psum(partial_sums[0].astype(jnp.bfloat16), "rep").astype(jnp.float32),
-        lax.psum(partial_sums[1].astype(jnp.bfloat16), "rep").astype(jnp.float32),
-        lax.psum(partial_sums[2].astype(jnp.bfloat16), "rep").astype(jnp.float32),
-        lax.psum(partial_sums[3].astype(jnp.bfloat16), "rep").astype(jnp.float32),
-        lax.psum(partial_sums[4].astype(jnp.bfloat16), "rep").astype(jnp.float32),
-        lax.psum(partial_sums[5].astype(jnp.bfloat16), "rep").astype(jnp.float32),
-        lax.psum(partial_sums[6].astype(jnp.bfloat16), "rep").astype(jnp.float32),
-        lax.psum(partial_sums[7].astype(jnp.bfloat16), "rep").astype(jnp.float32),
-        lax.psum(partial_sums[8].astype(jnp.bfloat16), "rep").astype(jnp.float32),
-        lax.psum(partial_sums[9].astype(jnp.bfloat16), "rep").astype(jnp.float32),
-        lax.psum(partial_sums[10].astype(jnp.bfloat16), "rep").astype(jnp.float32),
-    )
+    vector_grads = jnp.stack([
+        grad_media_gain, grad_media_bias, grad_latent_gain, grad_latent_bias, grad_feed_gain, grad_feed_bias])
+    weight_grads = [
+        g.astype(jnp.bfloat16) for g in (grad_query, grad_context, grad_output, grad_up, grad_down)]
+    if tiled:
+        summed, vector_sums = reduce_gradients(weight_grads, jnp.pad(vector_grads, ((0, 2), (0, 0))), chips // 4)
+        width = media_gain.shape[0]
+        mine = lax.dynamic_slice(vector_sums, (0, lax.axis_index("dp") * width), (6, width))
+        owned = tuple(mine) + tuple(summed)
+    else:
+        vector_sums = lax.psum_scatter(vector_grads, "dp", scatter_dimension=1, tiled=True)
+        summed = [lax.psum_scatter(g, "dp", scatter_dimension=0, tiled=True) for g in weight_grads]
+        owned = tuple(lax.psum(vector_sums, "rep")) + tuple(
+            lax.psum(s, "rep").astype(jnp.float32) for s in summed)
     return (
         latents_out,
         grad_media,

time: 1530 us -> 429 us (0.28)
  waiting for transfers between devices: 1140 us -> 0 us
  Pallas kernels: 0 us -> 253 us
  blocking collectives: 161 us -> 0 us
  other arithmetic: 47.5 us -> 23.6 us
  matrix products: 107 us -> 89 us
    reduce_scatter x5 -> x0, waiting for transfers between devices: 873 us -> none  [the longest x1 352 us: body(): lax.psum_scatter(grad_down, 'dp', scatter_dimension=0, tiled=True)]
    all_gather x5 -> x0, waiting for transfers between devices: 261 us -> none  [the longest x1 111 us: body(): lax.all_gather(up_weight, 'dp', axis=0, tiled=True)]
    pallas_call x0 -> x2, Pallas kernels: none -> 253 us  [the longest x1 129 us: gather_parameters(): pl.pallas_call(functools.partial(gather_kernel, length), out_shape=out_sh...]
    unnamed x2 -> x0, blocking collectives: 158 us -> none
    convert_element_type x17 -> x0, other arithmetic: 22.3 us -> none  [the longest x1 2.5 us: body(): (d_middle + d_latent_norm).astype(jnp.bfloat16).reshape(latents.shape)]
  transfers between devices with their start and end apart: 11 -> 0, of which waited for: 9 -> 0; matrix products, arithmetic and copies ran while one was open for 10% -> 0% of each run, Pallas kernels for 0% -> 0%
where the time goes in v1:
time: 429 us; the launch traced here: 423 us
  Pallas kernels  253 us (59%)
  matrix products  89 us (21%)
  local copies, waits for them, and re-layouts  54.9 us (13%)
  other arithmetic  23.6 us (6%)
    pallas_call x1, Pallas kernels, gather_parameters(): pl.pallas_call(functools.partial(gather_kernel, length), out_shape=out_sh...  129 us
    pallas_call x1, Pallas kernels, reduce_gradients(): pl.pallas_call(functools.partial(reduce_kernel, length), out_shape=([jax....  125 us
    dot_general x5, matrix products, matmul_left(): lax.dot_general(left, right, (((0,), (0,)), ((), ())), preferred_element_...  29.8 us
    dot_general x5, matrix products, matmul(): return jnp.dot(left, right, preferred_element_type=jnp.float32)  22.2 us
    dot_general x5, matrix products, matmul_right(): lax.dot_general(left, right, (((1,), (1,)), ((), ())), preferred_element_...  19.7 us
    unnamed x63, local copies, waits for them, and re-layouts  14.7 us

profile of v1, /device:TPU:0, one launch (start us, length us, event | category | flops | bytes accessed | tf_op | source)
XLA Modules:
  0.0 423.0 jit_solution(14768088159762116865)
XLA Ops:
  3.0 1.2 convert_reduce_fusion.1
  4.3 1.4 multiply_reduce_fusion.6
  5.8 2.2 convert_reduce_fusion
  10.0 128.6 %gather_parameters.1 = (bf16[4,2,2,2,32,512]{5,4,3,2,1,0:T(8,128)(2,1)}, bf16[4,2,2,2,32,1024]{5,4,3,2,1,0:T(8,128)(2,1)}, bf16[4,2,2,2,16,1024]{5,4,3,2,1,0:T(8...) custom-call(bf16[64,512]{1,0:T(8,128)(2,1)} %refs_0_.1, ...), custom_call_target="tpu_custom_call" | custom-call | tf_op jit(solution)/shard_map/gather_parameters/pallas_call | solution.py:387
  142.3 1.2 fusion.37
  143.5 2.2 reshape.540
  145.7 2.3 copy.42
  147.9 1.6 fusion.14
  152.1 3.7 convolution_convert_fusion.2
  155.8 2.0 fusion.52
  157.8 3.7 copy.38
  161.6 3.7 copy.37
  165.2 2.6 fusion.53
  167.8 1.2 fusion.16
  170.8 2.0 fusion.33
  172.8 2.2 copy.40
  175.0 2.2 reshape.542
  177.2 1.9 fusion.54
  179.5 8.9 %fusion.50 = f32[320,4096]{1,0:T(8,128)} fusion(bf16[1024,4096]{1,0:T(8,128)(2,1)} %bitcast.194, f32[320,1024]{1,0:T(8,128)S(1)} %get-tuple-element.72, f32[1024]{0:T(1024)S(1)} %reshape.575, f32[1024]{0:T(1024)S(1)} %reshape.574, f32[320]{0:T(512)S(1)} %fusion.46, f32[320]{0:T(512)S(1)} %broadcast_multiply_fusion.2), kind=kOutput, calls=%fused_computation.121 | convolution fusion | flops 2685992960 | bytes 14952960 | tf_op jit(solution)/shard_map/dot_general | solution.py:451
  188.4 8.4 %add_convert_fusion = (bf16[320,4096]{1,0:T(8,128)(2,1)S(1)}, bf16[320,4096]{1,0:T(8,128)(2,1)}) fusion(f32[320,4096]{1,0:T(8,128)} %fusion.50, bf16[320,1024]{1,0:T(8,128)(2,1)S(1)} %bitcast.175, bf16[4096,1024]{1,0:T(8,128)(2,1)S(1)} %bitcast.200), kind=kOutput, calls=%fused_computation.23 | convolution fusion | flops 2704015360 | bytes 19529728 | tf_op jit(solution)/shard_map/dot_general | solution.py:461
  196.9 6.4 %fusion.27 = bf16[320,1024]{1,0:T(8,128)(2,1)} fusion(f32[320,1024]{1,0:T(8,128)S(1)} %get-tuple-element.72, bf16[320,4096]{1,0:T(8,128)(2,1)} %get-tuple-element.56, bf16[4096,1024]{1,0:T(8,128)(2,1)S(1)} %bitcast.201, f32[320]{0:T(512)S(1)} %broadcast_in_dim.19), kind=kOutput, calls=%fused_computation.53 | convolution fusion | flops 2685337600 | bytes 12977408 | tf_op jit(solution)/shard_map/dot_general | solution.py:451
  203.3 3.2 multiply_reduce_fusion.1
  207.9 1.3 convolution_convert_fusion.7
  209.2 1.7 convolution_convert_fusion.4
  210.9 2.2 reshape.547
  213.1 2.3 copy.43
  215.4 4.4 %fusion.23 = bf16[5,8,64,320]{3,2,1,0:T(8,128)(2,1)} fusion(bf16[5,64,8,64]{1,3,2,0:T(8,128)(2,1)} %copy.43, f32[5,8,64,320]{3,2,1,0:T(8,128)} %copy-done, f32[5,8,64]{2,1,0:T(8,128)S(1)} %log_add_fusion), kind=kOutput, calls=%fused_computation.46 | convolution fusion | flops 107315200 | bytes 5253120 | tf_op jit(solution)/shard_map/bhqk,bqhd->bkhd/dot_general | solution.py:589
  219.8 3.9 copy.45
  223.7 4.6 %multiply_reduce_fusion = (f32[5,8,64]{2,1,0:T(8,128)S(1)}, f32[5,8,64,320]{3,2,1,0:T(8,128)S(1)}) fusion(f32[5,8,64,320]{3,2,1,0:T(8,128)} %copy-done, f32[5,8,64]{2,1,0:T(8,128)S(1)} %log_add_fusion, bf16[5,64,8,64]{1,3,2,0:T(8,128)(2,1)} %copy.43, bf16[5,320,8,64]{1,3,2,0:T(8,128)(2,1)} %bitcast.160), kind=kOutput, calls=%fused_computation.30 | convolution fusion | flops 107312640 | bytes 8540160 | tf_op jit(solution)/shard_map/bqhd,bkhd->bhqk/dot_general | solution.py:467
  229.9 1.7 fusion.35
  231.6 1.9 convolution_convert_fusion.3
  233.5 4.0 copy.44
  237.6 8.3 %bitcast_convert_fusion = bf16[1024,1024]{1,0:T(8,128)(2,1)} fusion(bf16[5,320,512]{2,1,0:T(8,128)(2,1)} %copy.45, bf16[5,320,512]{2,1,0:T(8,128)(2,1)} %copy.44, bf16[5,64,1024]{2,1,0:T(8,128)(2,1)} %fusion.32, bf16[5,256,1024]{2,1,0:T(8,128)(2,1)} %copy-done.8), kind=kOutput, calls=%fused_computation.28 | convolution fusion | flops 3369598976 | bytes 8650752 | tf_op jit(solution)/shard_map/dot_general | solution.py:455
  245.9 2.2 copy.46
  248.1 2.2 reshape.548
  250.4 2.9 convolution_convert_fusion.5
  253.2 5.9 %fusion.18 = f32[5,320,1024]{2,1,0:T(8,128)S(1)} fusion(bf16[1024,1024,1]{1,0,2:T(8,128)(2,1)} %bitcast.202, bf16[5,320,512]{2,1,0:T(8,128)(2,1)} %copy.45, bf16[5,320,512]{2,1,0:T(8,128)(2,1)} %copy.44), kind=kOutput, calls=%fused_computation.39 | convolution fusion | flops 3361996800 | bytes 11927552 | tf_op jit(solution)/shard_map/dot_general | solution.py:461
  259.2 1.1 fusion.4
  260.3 2.8 fusion.15
  263.3 3.1 fusion.6
  268.7 2.3 fusion.36
  271.6 10.2 %convolution_convert_fusion.1 = bf16[1024,4096]{1,0:T(8,128)(2,1)} fusion(bf16[320,4096]{1,0:T(8,128)(2,1)} %copy-done.23, f32[320,1024]{1,0:T(8,128)} %copy-done.7, f32[1024]{0:T(1024)S(1)} %reshape.575, f32[1024]{0:T(1024)S(1)} %reshape.574, f32[320]{0:T(512)S(1)} %fusion.46, f32[320]{0:T(512)S(1)} %broadcast_multiply_fusion.2), kind=kOutput, calls=%fused_computation.6 | convolution fusion | flops 2690187264 | bytes 12331520 | tf_op jit(solution)/shard_map/dot_general | solution.py:455
  281.9 6.7 %convolution_convert_fusion = bf16[4096,1024]{1,0:T(8,128)(2,1)} fusion(bf16[320,4096]{1,0:T(8,128)(2,1)S(1)} %copy-done.24, bf16[320,1024]{1,0:T(8,128)(2,1)S(1)} %get-tuple-element.59), kind=kOutput, calls=%fused_computation.5 | convolution fusion | flops 2688548864 | bytes 11665408 | tf_op jit(solution)/shard_map/dot_general | solution.py:455
  288.6 124.5 %reduce_gradients.1 = (f32[2,32,512]{2,1,0:T(8,128)}, f32[2,32,1024]{2,1,0:T(8,128)}, f32[2,16,1024]{2,1,0:T(8,128)}, f32[2,32,4096]{2,1,0:T(8,128)}, f32[2,128,1024]{2,1,0:T(8,128)}, /*index=5*/f32[8,1024]{1,0:T(8,128)}) custom-call(bf16[4,2,2,2,32,512]{5,4,3,2,1,0:T(8,128)(2,1)} %bitcast.171, bf16[4,2,2,2,32,1024]{5,4,3,2,1,0:T(8,128)(2,1)} %bitcast.167, ...), custom_call_target="tpu_custom_call" | custom-call | tf_op jit(solution)/shard_map/reduce_gradients/pallas_call | solution.py:426
  414.5 1.6 copy.53
  416.1 1.7 copy.54
  417.8 1.6 copy.55
  419.3 2.3 copy.56
  (107 shorter events, 20.2 us)
Async XLA Ops:
  0.6 7.4 %copy-start.2 = (bf16[1,5,256,1024]{3,2,1,0:T(8,128)(2,1)S(1)}, bf16[1,5,256,1024]{3,2,1,0:T(8,128)(2,1)}, u32[]{:S(2)}) copy-start(bf16[1,5,256,1024]{3,2,1,0:T(8,128)(2,1)} %param.15) | copy-start | bytes 7864324
  5.8 3.1 copy-start.10
  8.1 131.9 %copy-start.3 = (bf16[1,5,64,1024]{3,2,1,0:T(8,128)(2,1)S(1)}, bf16[1,5,64,1024]{3,2,1,0:T(8,128)(2,1)}, u32[]{:S(2)}) copy-start(bf16[1,5,64,1024]{3,2,1,0:T(8,128)(2,1)} %param.16) | copy-start | bytes 1966084
  139.9 2.3 copy-start.21
  141.4 0.8 copy-start.18
  147.9 1.6 copy-start.14
  149.5 1.6 copy-start.8
  149.5 2.5 copy-start.20
  167.8 2.0 copy-start
  167.8 3.0 copy-start.9
  179.2 27.3 %copy-start.7 = (f32[320,1024]{1,0:T(8,128)}, f32[320,1024]{1,0:T(8,128)S(1)}, u32[]{:S(2)}) copy-start(f32[320,1024]{1,0:T(8,128)S(1)} %get-tuple-element.72) | copy-start | bytes 3932164
  179.2 9.2 %slice-start.2 = ((s8[8388608]{0:T(1024)(128)(4,1)}), s8[4194304]{0:T(1024)(128)(4,1)S(1)}, s32[]{:S(2)}) async-start(s8[8388608]{0:T(1024)(128)(4,1)} %bitcast.198), calls=%async_computation.2 | async-start | bytes 8388608
  179.5 8.9 %copy-start.17 = (bf16[1,5,64,1024]{3,2,1,0:T(8,128)(2,1)S(1)}, bf16[1,5,64,1024]{3,2,1,0:T(8,128)(2,1)}, u32[]{:S(2)}) copy-start(bf16[1,5,64,1024]{3,2,1,0:T(8,128)(2,1)} %multiply_convert_fusion.2) | copy-start | bytes 1966084
  179.5 8.9 %slice-start.3 = ((s8[8388608]{0:T(1024)(128)(4,1)}), s8[4194304]{0:T(1024)(128)(4,1)S(1)}, s32[]{:S(2)}) async-start(s8[8388608]{0:T(1024)(128)(4,1)} %bitcast.198), calls=%async_computation.3 | async-start | bytes 8388608
  179.5 23.7 %slice-start = ((s8[8388608]{0:T(1024)(128)(4,1)}), s8[4194304]{0:T(1024)(128)(4,1)S(1)}, s32[]{:S(2)}) async-start(s8[8388608]{0:T(1024)(128)(4,1)} %bitcast.195), calls=%async_computation | async-start | bytes 8388608
  188.4 14.8 %slice-start.1 = ((s8[8388608]{0:T(1024)(128)(4,1)}), s8[4194304]{0:T(1024)(128)(4,1)S(1)}, s32[]{:S(2)}) async-start(s8[8388608]{0:T(1024)(128)(4,1)} %bitcast.195), calls=%async_computation.1 | async-start | bytes 8388608
  196.8 6.4 %copy-start.23 = (bf16[320,4096]{1,0:T(8,128)(2,1)}, bf16[320,4096]{1,0:T(8,128)(2,1)S(1)}, u32[]{:S(2)}) copy-start(bf16[320,4096]{1,0:T(8,128)(2,1)S(1)} %get-tuple-element.55) | copy-start | bytes 7864324
  206.5 1.1 copy-start.11
  206.5 1.4 copy-start.15
  207.0 3.9 copy-start.5
  207.0 2.2 copy-start.13
  223.7 4.6 %copy-start.1 = (f32[5,8,64,320]{3,2,1,0:T(8,128)S(1)}, f32[5,8,64,320]{3,2,1,0:T(8,128)}, u32[]{:S(2)}) copy-start(f32[5,8,64,320]{3,2,1,0:T(8,128)} %copy-done) | copy-start | bytes 9830404
  228.3 1.5 copy-start.4
  229.9 1.7 copy-start.12
  263.3 3.1 copy-start.19
  263.3 3.1 copy-start.22
  267.4 1.3 copy-start.6
  271.6 10.2 %copy-start.24 = (bf16[320,4096]{1,0:T(8,128)(2,1)S(1)}, bf16[320,4096]{1,0:T(8,128)(2,1)}, u32[]{:S(2)}) copy-start(bf16[320,4096]{1,0:T(8,128)(2,1)} %get-tuple-element.56) | copy-start | bytes 7864324
  413.1 8.5 %copy-start.16 = (f32[2,128,1024]{2,1,0:T(8,128)S(1)}, f32[2,128,1024]{2,1,0:T(8,128)}, u32[]{:S(2)}) copy-start(f32[2,128,1024]{2,1,0:T(8,128)} %get-tuple-element.37) | copy-start | bytes 3145732
